TPU v7x, 32 devices: a whole 2x2x4 slice. The times are simulated.
32 devices in a mesh: section: 4 (over y, x), tp: 8 (over z, core).
Axes of the slice: x: 2, y: 2, z: 4, core: 2. Of those that a mesh axis runs over, the one named last changes fastest.
Arguments:
- tokens: bfloat16 [64, 8192], P(None, 'tp'), may hold values from -6 to 6
- norm_gain: float32 [4, 8192], P('section'), may hold values from 0.1 to 1.9
- gate_weight: bfloat16 [4, 8192, 16384], P('section', None, 'tp'), may hold values from -0.09375 to 0.09375
- up_weight: bfloat16 [4, 8192, 16384], P('section', None, 'tp'), may hold values from -0.09375 to 0.09375
- gate_mask: int32 [4, 128, 256], P('section', None, 'tp'), may hold values 0 or 1
- up_mask: int32 [4, 128, 256], P('section', None, 'tp'), may hold values 0 or 1
- down_weight: bfloat16 [4, 16384, 8192], P('section', 'tp'), may hold values from -0.125 to 0.125
- down_mask: int32 [4, 256, 128], P('section', 'tp'), may hold values 0 or 1
- slot_order: int32 [4, 256], P('section', 'tp'), may hold values from 0 to 255, as said below
Outputs:
- received: bfloat16 [4, 64, 8192], P('section', None, 'tp')
Inputs may be any that keep to these rules, and one draw needn't show every extreme that they name: `slot_order`: for each section a permutation of the 256 hidden blocks. Slot k lies on tp device k // 32; block b is computed on tp device b // 32. The slots of tp device t take exactly 4 blocks from each of the tp devices t, t + 1, ..., t + 8 - 1 (mod 8) and none from others. `gate_mask`: 1 keeps a block, 0 prunes it. `up_mask`: 1 keeps a block, 0 prunes it. `down_mask`: 1 keeps a block, 0 prunes it.
All inputs are finite; a program needn't handle non-finite values.
Results may differ from a plain program's by a relative error of at most 0.014.
Values may be sent and summed in bfloat16 or wider, within the bound.
No kernel may reach another device: no remote copies, remote signals or barrier semaphores. Data moves between devices by JAX's collectives and lax.ppermute only.
A program may use at most 320 MiB of HBM per device.

v0:
```python
import jax
import jax.numpy as jnp
from jax import lax
from jax.sharding import PartitionSpec as P


def passed_along(block, axis, distance):
    devices = range(lax.axis_size(axis))
    route = [((i - distance) % len(devices), i) for i in devices]
    return lax.ppermute(block, axis, route)


def expand_mask(mask, width):
    return jnp.repeat(jnp.repeat(mask, width, axis=0), width, axis=1)


def masked(weight, mask, width):
    return weight * expand_mask(mask, width).astype(jnp.bfloat16)


def body(
    tokens,
    norm_gain,
    gate_weight,
    up_weight,
    gate_mask,
    up_mask,
    down_weight,
    down_mask,
    slot_order,
):
    sections = lax.axis_size("section")
    tp_count = lax.axis_size("tp")
    section_pos = lax.axis_index("section")
    tp_pos = lax.axis_index("tp")
    width = gate_weight.shape[1] // gate_mask.shape[1]
    w_gate = masked(gate_weight[0], gate_mask[0], width)
    w_up = masked(up_weight[0], up_mask[0], width)
    w_down = masked(down_weight[0], down_mask[0], width)
    gain = norm_gain[0]
    my_blocks = slot_order[0]
    per_device = my_blocks.shape[0]
    row_count, own_cols = tokens.shape
    window = min(tp_count, per_device)
    capacity = per_device // window
    slot_ids = jnp.arange(capacity, dtype=jnp.int32)
    my_source = my_blocks // per_device
    my_offset = (my_source - tp_pos) % tp_count
    lanes = jnp.arange(per_device, dtype=jnp.int32)
    earlier = (my_source[None, :] == my_source[:, None]) & (lanes[None, :] < lanes[:, None])
    my_rank = jnp.sum(earlier.astype(jnp.int32), axis=1)
    send_lists = []
    for offset in range(window):
        if offset == 0:
            table_row = my_blocks
        else:
            table_row = passed_along(my_blocks, "tp", offset)
        row_source = table_row // per_device
        row_block = table_row % per_device
        from_me = (row_source == tp_pos).astype(jnp.int32)
        order_rank = jnp.cumsum(from_me) - 1
        picks = (from_me[None, :] == 1) & (order_rank[None, :] == slot_ids[:, None])
        send_lists.append(jnp.sum(jnp.where(picks, row_block[None, :], 0), axis=1))
    x_full = lax.all_gather(tokens, "tp", axis=1, tiled=True)
    saved = jnp.zeros((row_count, own_cols), jnp.bfloat16)
    for round_pos in range(sections):
        x_own = lax.dynamic_slice_in_dim(x_full, tp_pos * own_cols, own_cols, 1)
        widened = x_full.astype(jnp.float32)
        scale = lax.rsqrt(jnp.mean(widened * widened, axis=-1, keepdims=True) + 1e-05)
        normed = (widened * scale * gain).astype(jnp.bfloat16)
        gate = jnp.dot(normed, w_gate, preferred_element_type=jnp.float32)
        upper = jnp.dot(normed, w_up, preferred_element_type=jnp.float32)
        hidden = (jax.nn.silu(gate) * upper).astype(jnp.bfloat16)
        flat = (
            hidden.reshape(row_count, per_device, width)
            .transpose(1, 0, 2)
            .reshape(per_device, row_count * width)
        )
        arrivals = []
        for gather_offset in range(window):
            outgoing = flat[send_lists[gather_offset]]
            if gather_offset == 0:
                arrivals.append(outgoing)
            else:
                arrivals.append(passed_along(outgoing, "tp", tp_count - gather_offset))
        stacked = jnp.stack(arrivals)
        chosen = stacked[my_offset, my_rank]
        mine = (
            chosen.reshape(per_device, row_count, width)
            .transpose(1, 0, 2)
            .reshape(row_count, per_device * width)
        )
        partial_sum = jnp.dot(mine, w_down, preferred_element_type=jnp.float32)
        summed = lax.psum_scatter(partial_sum, "tp", scatter_dimension=1, tiled=True)
        y_own = (x_own.astype(jnp.float32) + summed).astype(jnp.bfloat16)
        got_own = passed_along(y_own, "section", 1)
        if round_pos + 1 < sections:
            x_full = lax.all_gather(got_own, "tp", axis=1, tiled=True)
        saved = jnp.where(section_pos == (round_pos + 1) % sections, got_own, saved)
    return saved[None]


def solution(mesh):
    return jax.shard_map(
        body,
        mesh=mesh,
        in_specs=(
            P(None, "tp"),
            P("section", None),
            P("section", None, "tp"),
            P("section", None, "tp"),
            P("section", None, "tp"),
            P("section", None, "tp"),
            P("section", "tp", None),
            P("section", "tp", None),
            P("section", "tp"),
        ),
        out_specs=P("section", None, "tp"),
        check_vma=False,
    )
```

profile of v0, /device:TPU:0, one launch (start us, length us, event | category | flops | bytes accessed | tf_op | source)
XLA Modules:
  0.0 736.9 jit_solution(2413459440024535056)
XLA Ops:
  7.0 3.9 collective-permute-start.4
  16.9 40.1 %copy.85 = bf16[1,8192,2048]{1,2,0:T(8,128)(2,1)} copy(bf16[1,8192,2048]{2,1,0:T(8,128)(2,1)} %param.11) | data formatting | bytes 67108864 | tf_op args[2]
  58.4 40.0 %copy.86 = bf16[1,8192,2048]{1,2,0:T(8,128)(2,1)} copy(bf16[1,8192,2048]{2,1,0:T(8,128)(2,1)} %param.12) | data formatting | bytes 67108864 | tf_op args[3]
  100.2 44.5 %copy.105 = bf16[1,2048,8192]{1,2,0:T(8,128)(2,1)} copy(bf16[1,2048,8192]{2,1,0:T(8,128)(2,1)} %param.15) | data formatting | bytes 67108864 | tf_op args[6]
  145.0 23.2 %bitcast_multiply_fusion.2 = bf16[8192,2048]{0,1:T(8,128)(2,1)} fusion(bf16[1,8192,2048]{1,2,0:T(8,128)(2,1)} %copy.85, bf16[8192,32]{0,1:T(8,128)(2,1)S(1)} %convert_element_type.149), kind=kLoop, calls=%fused_computation.46 | loop fusion | flops 16777216 | bytes 67633152 | tf_op jit(solution)/shard_map/mul | solution.py:18
  168.5 23.2 %bitcast_multiply_fusion.1 = bf16[8192,2048]{0,1:T(8,128)(2,1)} fusion(bf16[1,8192,2048]{1,2,0:T(8,128)(2,1)} %copy.86, bf16[8192,32]{0,1:T(8,128)(2,1)S(1)} %convert_element_type.153), kind=kLoop, calls=%fused_computation.45 | loop fusion | flops 16777216 | bytes 67633152 | tf_op jit(solution)/shard_map/mul | solution.py:18
  191.7 23.5 %bitcast_multiply_fusion = bf16[1,2048,8192]{1,2,0:T(8,128)(2,1)} fusion(bf16[1,2048,8192]{1,2,0:T(8,128)(2,1)} %copy.105, bf16[2048,128]{0,1:T(8,128)(2,1)S(1)} %copy.104), kind=kLoop, calls=%fused_computation.44 | loop fusion | flops 16777216 | bytes 67633152 | tf_op jit(solution)/shard_map/mul | solution.py:18
  223.9 15.3 %fusion.34 = f32[64,2048]{1,0:T(8,128)S(1)} fusion(bf16[8192,2048]{0,1:T(8,128)(2,1)} %bitcast_multiply_fusion.2, bf16[64,8192]{1,0:T(8,128)(2,1)} %all-gather.5.cloned.1.call-done, f32[8192]{0:T(1024)S(1)} %bitcast.175, f32[64]{0:T(128)S(1)} %add_rsqrt_fusion.3), kind=kOutput, calls=%fused_computation.82 | convolution fusion | flops 2149580800 | bytes 35160320 | tf_op jit(solution)/shard_map/dot_general | solution.py:71
  239.3 15.6 %fusion.8 = bf16[64,2048]{1,0:T(8,128)(2,1)S(1)} fusion(bf16[8192,2048]{0,1:T(8,128)(2,1)} %bitcast_multiply_fusion.1, f32[64,2048]{1,0:T(8,128)S(1)} %fusion.34, bf16[64,8192]{1,0:T(8,128)(2,1)S(1)} %copy-done, f32[8192]{0:T(1024)S(1)} %bitcast.176, f32[64]{0:T(128)S(1)} %add_rsqrt_fusion.3), kind=kOutput, calls=%fused_computation.59 | convolution fusion | flops 2150367232 | bytes 35422464 | tf_op jit(solution)/shard_map/dot_general | solution.py:72
  258.6 3.0 collective-permute-start.3
  270.6 2.8 collective-permute-done.11
  276.3 16.1 %fusion.6 = f32[64,8192]{1,0:T(8,128)} fusion(bf16[64,2048]{1,0:T(8,128)(2,1)S(1)} %reshape.607, bf16[1,2048,8192]{1,2,0:T(8,128)(2,1)} %bitcast_multiply_fusion), kind=kOutput, calls=%fused_computation.42 | convolution fusion | flops 2147483648 | bytes 35913728 | tf_op jit(solution)/shard_map/dot_general | solution.py:93
  292.5 34.8 %reduce-scatter.5.cloned.1.call-done = f32[64,1024]{1,0:T(8,128)} async-done(((f32[64,8192]{1,0:T(8,128)}), f32[64,1024]{1,0:T(8,128)}) %reduce-scatter.5.cloned.1.call-update) | async-done | bytes 262160 | tf_op jit(solution)/shard_map/reduce_scatter | solution.py:94
  329.9 4.4 collective-permute-done.14
  334.9 19.6 %all-gather.7.cloned.1.call-done = bf16[64,8192]{1,0:T(8,128)(2,1)} async-done(((bf16[64,1024]{1,0:T(8,128)(2,1)}), bf16[64,8192]{1,0:T(8,128)(2,1)}) %all-gather.7.cloned.1.call-update) | async-done | bytes 1048592 | tf_op jit(solution)/shard_map/all_gather | solution.py:98
  356.1 15.3 %fusion.31 = f32[64,2048]{1,0:T(8,128)S(1)} fusion(bf16[8192,2048]{0,1:T(8,128)(2,1)} %bitcast_multiply_fusion.2, bf16[64,8192]{1,0:T(8,128)(2,1)} %all-gather.7.cloned.1.call-done, f32[64]{0:T(128)S(1)} %add_rsqrt_fusion.2, f32[8192]{0:T(1024)S(1)} %bitcast.177), kind=kOutput, calls=%fused_computation.81 | convolution fusion | flops 2149580800 | bytes 35160320 | tf_op jit(solution)/shard_map/dot_general | solution.py:71
  371.4 15.6 %fusion.9 = bf16[64,2048]{1,0:T(8,128)(2,1)S(1)} fusion(bf16[8192,2048]{0,1:T(8,128)(2,1)} %bitcast_multiply_fusion.1, f32[64,2048]{1,0:T(8,128)S(1)} %fusion.31, bf16[64,8192]{1,0:T(8,128)(2,1)S(1)} %copy-done.2, f32[64]{0:T(128)S(1)} %add_rsqrt_fusion.2, f32[8192]{0:T(1024)S(1)} %bitcast.178), kind=kOutput, calls=%fused_computation.60 | convolution fusion | flops 2150367232 | bytes 35422464 | tf_op jit(solution)/shard_map/dot_general | solution.py:72
  409.0 16.1 %fusion.4 = f32[64,8192]{1,0:T(8,128)} fusion(bf16[64,2048]{1,0:T(8,128)(2,1)S(1)} %reshape.611, bf16[1,2048,8192]{1,2,0:T(8,128)(2,1)} %bitcast_multiply_fusion), kind=kOutput, calls=%fused_computation.40 | convolution fusion | flops 2147483648 | bytes 35913728 | tf_op jit(solution)/shard_map/dot_general | solution.py:93
  425.2 34.1 %reduce-scatter.7.cloned.1.call-done = f32[64,1024]{1,0:T(8,128)} async-done(((f32[64,8192]{1,0:T(8,128)}), f32[64,1024]{1,0:T(8,128)}) %reduce-scatter.7.cloned.1.call-update) | async-done | bytes 262160 | tf_op jit(solution)/shard_map/reduce_scatter | solution.py:94
  461.7 4.5 collective-permute-done.22
  466.9 19.4 %all-gather.9.cloned.1.call-done = bf16[64,8192]{1,0:T(8,128)(2,1)} async-done(((bf16[64,1024]{1,0:T(8,128)(2,1)}), bf16[64,8192]{1,0:T(8,128)(2,1)}) %all-gather.9.cloned.1.call-update) | async-done | bytes 1048592 | tf_op jit(solution)/shard_map/all_gather | solution.py:98
  487.8 15.3 %fusion.28 = f32[64,2048]{1,0:T(8,128)S(1)} fusion(bf16[8192,2048]{0,1:T(8,128)(2,1)} %bitcast_multiply_fusion.2, bf16[64,8192]{1,0:T(8,128)(2,1)} %all-gather.9.cloned.1.call-done, f32[64]{0:T(128)S(1)} %add_rsqrt_fusion.1, f32[8192]{0:T(1024)S(1)} %bitcast.179), kind=kOutput, calls=%fused_computation.80 | convolution fusion | flops 2149580800 | bytes 35160320 | tf_op jit(solution)/shard_map/dot_general | solution.py:71
  503.2 15.6 %fusion.10 = bf16[64,2048]{1,0:T(8,128)(2,1)S(1)} fusion(bf16[8192,2048]{0,1:T(8,128)(2,1)} %bitcast_multiply_fusion.1, f32[64,2048]{1,0:T(8,128)S(1)} %fusion.28, bf16[64,8192]{1,0:T(8,128)(2,1)S(1)} %copy-done.3, f32[64]{0:T(128)S(1)} %add_rsqrt_fusion.1, f32[8192]{0:T(1024)S(1)} %bitcast.180), kind=kOutput, calls=%fused_computation.61 | convolution fusion | flops 2150367232 | bytes 35422464 | tf_op jit(solution)/shard_map/dot_general | solution.py:72
  540.5 16.1 %fusion.2 = f32[64,8192]{1,0:T(8,128)} fusion(bf16[64,2048]{1,0:T(8,128)(2,1)S(1)} %reshape.615, bf16[1,2048,8192]{1,2,0:T(8,128)(2,1)} %bitcast_multiply_fusion), kind=kOutput, calls=%fused_computation.38 | convolution fusion | flops 2147483648 | bytes 35913728 | tf_op jit(solution)/shard_map/dot_general | solution.py:93
  556.7 34.0 %reduce-scatter.9.cloned.1.call-done = f32[64,1024]{1,0:T(8,128)} async-done(((f32[64,8192]{1,0:T(8,128)}), f32[64,1024]{1,0:T(8,128)}) %reduce-scatter.9.cloned.1.call-update) | async-done | bytes 262160 | tf_op jit(solution)/shard_map/reduce_scatter | solution.py:94
  593.2 4.4 collective-permute-done.30
  598.3 19.4 %all-gather.11.cloned.1.call-done = bf16[64,8192]{1,0:T(8,128)(2,1)} async-done(((bf16[64,1024]{1,0:T(8,128)(2,1)}), bf16[64,8192]{1,0:T(8,128)(2,1)}) %all-gather.11.cloned.1.call-update) | async-done | bytes 1048592 | tf_op jit(solution)/shard_map/all_gather | solution.py:98
  619.3 15.3 %fusion.25 = f32[64,2048]{1,0:T(8,128)S(1)} fusion(bf16[8192,2048]{0,1:T(8,128)(2,1)} %bitcast_multiply_fusion.2, bf16[64,8192]{1,0:T(8,128)(2,1)} %all-gather.11.cloned.1.call-done, f32[64]{0:T(128)S(1)} %add_rsqrt_fusion, f32[8192]{0:T(1024)S(1)} %bitcast.181), kind=kOutput, calls=%fused_computation.79 | convolution fusion | flops 2149580800 | bytes 35160320 | tf_op jit(solution)/shard_map/dot_general | solution.py:71
  634.6 15.6 %fusion.11 = bf16[64,2048]{1,0:T(8,128)(2,1)S(1)} fusion(bf16[8192,2048]{0,1:T(8,128)(2,1)} %bitcast_multiply_fusion.1, f32[64,2048]{1,0:T(8,128)S(1)} %fusion.25, bf16[64,8192]{1,0:T(8,128)(2,1)S(1)} %copy-done.1, f32[64]{0:T(128)S(1)} %add_rsqrt_fusion, f32[8192]{0:T(1024)S(1)} %bitcast.182), kind=kOutput, calls=%fused_computation.62 | convolution fusion | flops 2150367232 | bytes 35422464 | tf_op jit(solution)/shard_map/dot_general | solution.py:72
  671.9 16.2 %fusion = f32[64,8192]{1,0:T(8,128)} fusion(bf16[64,2048]{1,0:T(8,128)(2,1)S(1)} %reshape.619, bf16[1,2048,8192]{1,2,0:T(8,128)(2,1)} %bitcast_multiply_fusion), kind=kOutput, calls=%fused_computation.36 | convolution fusion | flops 2147483648 | bytes 35913728 | tf_op jit(solution)/shard_map/dot_general | solution.py:93
  688.1 34.2 %reduce-scatter.11.cloned.1.call-done = f32[64,1024]{1,0:T(8,128)} async-done(((f32[64,8192]{1,0:T(8,128)}), f32[64,1024]{1,0:T(8,128)}) %reduce-scatter.11.cloned.1.call-update) | async-done | bytes 262160 | tf_op jit(solution)/shard_map/reduce_scatter | solution.py:94
  724.8 4.4 collective-permute-done.38
  (298 shorter events, 116.6 us)
Async XLA Ops:
  6.5 215.8 %all-gather.5.cloned.1.call-start = ((), (), s32[]{:S(2)}) async-start(), calls=%async_computation.4 | async-start | bytes 1179648 | tf_op jit(solution)/shard_map/all_gather | solution.py:64
  6.5 208.6 %collective-permute-start = (s32[32]{0:T(128)}, s32[32]{0:T(128)S(1)}, u32[]{:S(2)}, u32[]{:S(2)}) collective-permute-start(s32[32]{0:T(128)} %bitcast.192), channel_id=1, source_target_pairs={{7,0},{0,1},{1,2},{2,3},{3,4},{4,5},{5,6},{6,7},{15,8},{8,9},{9,10... | collective-permute-start | bytes 392 | tf_op jit(solution)/shard_map/ppermute | solution.py:10
  7.0 210.3 %collective-permute-start.4 = (s32[32]{0:T(128)}, s32[32]{0:T(128)S(1)}, u32[]{:S(2)}, u32[]{:S(2)}) collective-permute-start(s32[32]{0:T(128)} %bitcast.193), channel_id=1, source_target_pairs={{5,0},{6,1},{7,2},{0,3},{1,4},{2,5},{3,6},{4,7},{13,8},{14,9},{15,... | collective-permute-start | bytes 392 | tf_op jit(solution)/shard_map/ppermute | solution.py:10
  10.9 209.0 %collective-permute-start.2 = (s32[32]{0:T(128)}, s32[32]{0:T(128)S(1)}, u32[]{:S(2)}, u32[]{:S(2)}) collective-permute-start(s32[32]{0:T(128)} %bitcast.194), channel_id=1, source_target_pairs={{6,0},{7,1},{0,2},{1,3},{2,4},{3,5},{4,6},{5,7},{14,8},{15,9},{8,1... | collective-permute-start | bytes 392 | tf_op jit(solution)/shard_map/ppermute | solution.py:10
  12.4 207.7 %collective-permute-start.8 = (s32[32]{0:T(128)}, s32[32]{0:T(128)S(1)}, u32[]{:S(2)}, u32[]{:S(2)}) collective-permute-start(s32[32]{0:T(128)} %bitcast.195), channel_id=1, source_target_pairs={{3,0},{4,1},{5,2},{6,3},{7,4},{0,5},{1,6},{2,7},{11,8},{12,9},{13,... | collective-permute-start | bytes 392 | tf_op jit(solution)/shard_map/ppermute | solution.py:10
  12.4 208.1 %collective-permute-start.6 = (s32[32]{0:T(128)}, s32[32]{0:T(128)S(1)}, u32[]{:S(2)}, u32[]{:S(2)}) collective-permute-start(s32[32]{0:T(128)} %bitcast.196), channel_id=1, source_target_pairs={{4,0},{5,1},{6,2},{7,3},{0,4},{1,5},{2,6},{3,7},{12,8},{13,9},{14,... | collective-permute-start | bytes 392 | tf_op jit(solution)/shard_map/ppermute | solution.py:10
  14.5 312.8 %reduce-scatter.5.cloned.1.call-start = ((), (), s32[]{:S(2)}) async-start(), calls=%async_computation.5 | async-start | bytes 2359296 | tf_op jit(solution)/shard_map/reduce_scatter | solution.py:94
  215.2 6.2 collective-permute-start.12
  257.3 10.3 %collective-permute-start.1 = (bf16[4,4096]{1,0:T(4,128)(2,1)S(1)}, bf16[4,4096]{1,0:T(4,128)(2,1)S(1)}, u32[]{:S(2)}, u32[]{:S(2)}) collective-permute-start(bf16[4,4096]{1,0:T(4,128)(2,1)S(1)} %gather_fusion.1), channel_id=1, source_target_pairs={{1,0},{2,1},{3,2},{4,3},{5,4},{6,5},{7,6},{0,7},{9,8},{10,9},{11,1... | collective-permute-start | bytes 98312 | tf_op jit(solution)/shard_map/ppermute | solution.py:10
  258.6 9.3 %collective-permute-start.3 = (bf16[4,4096]{1,0:T(4,128)(2,1)S(1)}, bf16[4,4096]{1,0:T(4,128)(2,1)S(1)}, u32[]{:S(2)}, u32[]{:S(2)}) collective-permute-start(bf16[4,4096]{1,0:T(4,128)(2,1)S(1)} %gather_fusion.2), channel_id=1, source_target_pairs={{2,0},{3,1},{4,2},{5,3},{6,4},{7,5},{0,6},{1,7},{10,8},{11,9},{12,... | collective-permute-start | bytes 98312 | tf_op jit(solution)/shard_map/ppermute | solution.py:10
  262.3 6.1 collective-permute-start.5
  267.5 5.9 collective-permute-start.11
  292.4 62.1 %all-gather.7.cloned.1.call-start = ((), (), s32[]{:S(2)}) async-start(), calls=%async_computation.6 | async-start | bytes 1179648 | tf_op jit(solution)/shard_map/all_gather | solution.py:98
  328.3 5.9 collective-permute-start.14
  334.9 124.4 %reduce-scatter.7.cloned.1.call-start = ((), (), s32[]{:S(2)}) async-start(), calls=%async_computation.7 | async-start | bytes 2359296 | tf_op jit(solution)/shard_map/reduce_scatter | solution.py:94
  389.4 8.9 %collective-permute-start.15 = (bf16[4,4096]{1,0:T(4,128)(2,1)S(1)}, bf16[4,4096]{1,0:T(4,128)(2,1)S(1)}, u32[]{:S(2)}, u32[]{:S(2)}) collective-permute-start(bf16[4,4096]{1,0:T(4,128)(2,1)S(1)} %gather_fusion.10), channel_id=1, source_target_pairs={{1,0},{2,1},{3,2},{4,3},{5,4},{6,5},{7,6},{0,7},{9,8},{10,9},{11,1... | collective-permute-start | bytes 98312 | tf_op jit(solution)/shard_map/ppermute | solution.py:10
  394.8 5.8 collective-permute-start.16
  396.6 6.2 collective-permute-start.18
  398.3 5.7 collective-permute-start.20
  425.1 61.1 %all-gather.9.cloned.1.call-start = ((), (), s32[]{:S(2)}) async-start(), calls=%async_computation.8 | async-start | bytes 1179648 | tf_op jit(solution)/shard_map/all_gather | solution.py:98
  460.2 5.9 collective-permute-start.22
  466.8 123.8 %reduce-scatter.9.cloned.1.call-start = ((), (), s32[]{:S(2)}) async-start(), calls=%async_computation.9 | async-start | bytes 2359296 | tf_op jit(solution)/shard_map/reduce_scatter | solution.py:94
  521.2 8.9 %collective-permute-start.23 = (bf16[4,4096]{1,0:T(4,128)(2,1)S(1)}, bf16[4,4096]{1,0:T(4,128)(2,1)S(1)}, u32[]{:S(2)}, u32[]{:S(2)}) collective-permute-start(bf16[4,4096]{1,0:T(4,128)(2,1)S(1)} %gather_fusion.19), channel_id=1, source_target_pairs={{1,0},{2,1},{3,2},{4,3},{5,4},{6,5},{7,6},{0,7},{9,8},{10,9},{11,1... | collective-permute-start | bytes 98312 | tf_op jit(solution)/shard_map/ppermute | solution.py:10
  526.6 5.8 collective-permute-start.24
  528.3 6.2 collective-permute-start.26
  556.6 61.1 %all-gather.11.cloned.1.call-start = ((), (), s32[]{:S(2)}) async-start(), calls=%async_computation.10 | async-start | bytes 1179648 | tf_op jit(solution)/shard_map/all_gather | solution.py:98
  591.6 5.9 collective-permute-start.30
  598.2 124.0 %reduce-scatter.11.cloned.1.call-start = ((), (), s32[]{:S(2)}) async-start(), calls=%async_computation.11 | async-start | bytes 2359296 | tf_op jit(solution)/shard_map/reduce_scatter | solution.py:94
  652.6 8.7 %collective-permute-start.31 = (bf16[4,4096]{1,0:T(4,128)(2,1)S(1)}, bf16[4,4096]{1,0:T(4,128)(2,1)S(1)}, u32[]{:S(2)}, u32[]{:S(2)}) collective-permute-start(bf16[4,4096]{1,0:T(4,128)(2,1)S(1)} %gather_fusion.28), channel_id=1, source_target_pairs={{1,0},{2,1},{3,2},{4,3},{5,4},{6,5},{7,6},{0,7},{9,8},{10,9},{11,1... | collective-permute-start | bytes 98312 | tf_op jit(solution)/shard_map/ppermute | solution.py:10
  659.6 6.2 collective-permute-start.34
  661.3 5.8 collective-permute-start.36
  723.2 5.9 collective-permute-start.38
  (30 other events, 421.7 us)
Sparse Core Ops, SparseCore 0:
  14.7 22.3 all-gather.4
  292.5 34.7 reduce-scatter.4
  335.0 19.4 all-gather.6
  425.2 33.9 reduce-scatter.6
  467.0 19.2 all-gather.8
  556.8 33.8 reduce-scatter.8
  598.4 19.3 all-gather.10
  688.2 33.9 reduce-scatter.10
where the time goes:
time: 749 us; the launch traced here: 737 us
  waiting for transfers between devices  233 us (31%)
  matrix products  188 us (25%)
  local copies, waits for them, and re-layouts  166 us (22%)
  other arithmetic  85.5 us (11%)
  starting transfers between devices  49.6 us (7%)
  between operations  14.6 us (2%)
    reduce_scatter x4, waiting for transfers between devices, body(): lax.psum_scatter(partial_sum, 'tp', scatter_dimension=1, tiled=True)  137 us
    unnamed x61, local copies, waits for them, and re-layouts  127 us
    mul x3, other arithmetic, masked(): return weight * expand_mask(mask, width).astype(jnp.bfloat16)  69.9 us
    dot_general x4, matrix products, body(): partial_sum = jnp.dot(mine, w_down, preferred_element_type=jnp.float32)  64.6 us
    dot_general x4, matrix products, body(): upper = jnp.dot(normed, w_up, preferred_element_type=jnp.float32)  62.5 us
    dot_general x4, matrix products, body(): gate = jnp.dot(normed, w_gate, preferred_element_type=jnp.float32)  61.3 us
    all_gather x3, waiting for transfers between devices, body(): x_full = lax.all_gather(got_own, 'tp', axis=1, tiled=True)  58.4 us
    ppermute x39, starting transfers between devices, passed_along(): return lax.ppermute(block, axis, route)  49.3 us
  transfers between devices with their start and end apart: 47, of which 26 were waited for; matrix products, arithmetic and copies ran while one was open for 30% of the time, Pallas kernels for 0%

commit v1 on v0

--- a/solution.py
+++ b/solution.py
@@ -1,6 +1,10 @@
+import functools
+
 import jax
 import jax.numpy as jnp
 from jax import lax
+from jax.experimental import pallas as pl
+from jax.experimental.pallas import tpu as pltpu
 from jax.sharding import PartitionSpec as P
 
 
@@ -18,7 +22,7 @@
     return weight * expand_mask(mask, width).astype(jnp.bfloat16)
 
 
-def body(
+def ring_body(
     tokens,
     norm_gain,
     gate_weight,
@@ -100,9 +104,315 @@
     return saved[None]
 
 
+BF = jnp.bfloat16
+F32 = jnp.float32
+VM = pl.BlockSpec(memory_space=pltpu.VMEM)
+SM = pl.BlockSpec(memory_space=pltpu.SMEM)
+HB = pl.BlockSpec(memory_space=pl.ANY)
+MIB = 2**20
+
+
+def place(load_pair, first, second):
+    lanes = lax.broadcasted_iota(jnp.int32, (1, 128), 1)
+    left = pltpu.roll(load_pair(first // 2), 64 * (first % 2), 1)
+    right = pltpu.roll(load_pair(second // 2), 64 * (1 - second % 2), 1)
+    return jnp.where(lanes < 64, left, right).astype(BF)
+
+
+def gate_up_kernel(
+    tile, slots, me_ref, send_ref, x_ref, gain_ref, gm_ref, um_ref, wg, wu, out_ref,
+    buf, sem, normed, masks, acc,
+):
+    pieces, rows, cols = x_ref.shape
+    depth, hid = wg.shape[1], wg.shape[2]
+    blocks = gm_ref.shape[1]
+    width = hid // blocks
+    per = cols // tile
+    steps = pieces * per
+    kept = tile // width
+    me = me_ref[0]
+
+    def source(piece):
+        half = pieces // 2
+        return me ^ (piece // half + 2 * (piece % half))
+
+    def start_row(step):
+        return pl.multiple_of(source(step // per) * cols + (step % per) * tile, tile)
+
+    def copies(step, slot):
+        return [
+            pltpu.make_async_copy(
+                w.at[0, pl.ds(start_row(step), tile)], buf.at[slot, j], sem.at[slot, j]
+            )
+            for j, w in enumerate((wg, wu))
+        ]
+
+    for step in range(slots):
+        for copy in copies(step, step):
+            copy.start()
+    spread = (
+        lax.broadcasted_iota(jnp.int32, (blocks, hid), 0)
+        == lax.broadcasted_iota(jnp.int32, (blocks, hid), 1) // width
+    ).astype(BF)
+    for j, mask in enumerate((gm_ref, um_ref)):
+        masks[j] = jnp.dot(mask[...].astype(F32).astype(BF), spread, preferred_element_type=F32)
+    total = jnp.zeros((rows, 1), F32)
+    for piece in range(pieces):
+        wide = x_ref[piece].astype(F32)
+        total = total + jnp.sum(wide * wide, axis=1, keepdims=True)
+    scale = lax.rsqrt(total / depth + 1e-05)
+    for piece in range(pieces):
+        gain = gain_ref[:, pl.ds(pl.multiple_of(source(piece) * cols, cols), cols)]
+        normed[piece] = (x_ref[piece].astype(F32) * scale * gain).astype(BF)
+    acc[...] = jnp.zeros_like(acc)
+
+    def step_body(step, carry):
+        slot = lax.rem(step, slots)
+        part = pl.multiple_of((step % per) * tile, tile)
+        x_part = normed[step // per, :, pl.ds(part, tile)]
+        mask_row = pl.multiple_of(start_row(step) // width, kept)
+        for j, copy in enumerate(copies(step, slot)):
+            copy.wait()
+            mask = masks[j, pl.ds(mask_row, kept), :].astype(BF)
+            weight = (buf[slot, j].reshape(kept, width, hid) * mask[:, None, :]).reshape(tile, hid)
+            acc[j] += jnp.dot(x_part, weight, preferred_element_type=F32)
+
+        @pl.when(step + slots < steps)
+        def _():
+            for copy in copies(step + slots, slot):
+                copy.start()
+
+        return carry
+
+    lax.fori_loop(0, steps, step_body, 0)
+    gate = acc[0]
+    hidden = (gate / (1.0 + jnp.exp(-gate)) * acc[1]).astype(BF)
+    acc[0] = hidden.astype(F32)
+
+    def load_pair(pair):
+        return acc[0, :, pl.ds(pl.multiple_of(pair * 128, 128), 128)]
+
+    each = out_ref.shape[2] // 128
+    for piece in range(pieces):
+        for pair in range(each):
+            at = piece * 2 * each + 2 * pair
+            out_ref[piece, :, pl.ds(pair * 128, 128)] = place(
+                load_pair, send_ref[at], send_ref[at + 1]
+            )
+
+
+def gate_up(me, send, x, gain, gate_mask, up_mask, w_gate, w_up):
+    pieces, rows, cols = x.shape
+    depth, hid = w_gate.shape[1:]
+    tile, slots = 512, 4
+    return pl.pallas_call(
+        functools.partial(gate_up_kernel, tile, slots),
+        in_specs=[SM, SM, VM, VM, VM, VM, HB, HB],
+        out_specs=VM,
+        out_shape=jax.ShapeDtypeStruct((pieces, rows, hid // pieces), BF),
+        scratch_shapes=[
+            pltpu.VMEM((slots, 2, tile, hid), BF),
+            pltpu.SemaphoreType.DMA((slots, 2)),
+            pltpu.VMEM((pieces, rows, cols), BF),
+            pltpu.VMEM((2, gate_mask.shape[0], hid), F32),
+            pltpu.VMEM((2, rows, hid), F32),
+        ],
+        compiler_params=pltpu.CompilerParams(vmem_limit_bytes=32 * MIB),
+        cost_estimate=pl.CostEstimate(
+            flops=4 * rows * depth * hid, bytes_accessed=4 * depth * hid, transcendentals=0
+        ),
+        name="gate_up",
+    )(me, send, x, gain, gate_mask, up_mask, w_gate, w_up)
+
+
+def down_kernel(
+    tile, slots, me_ref, take_ref, arrived, x_ref, mask_ref, wd, keep_ref, pass_ref,
+    buf, sem, mine,
+):
+    pieces, rows, share = arrived.shape
+    hid = wd.shape[1]
+    cols = wd.shape[2] // pieces
+    blocks, out_blocks = mask_ref.shape
+    width = hid // blocks
+    per = cols // tile
+    steps = pieces * per
+    half = pieces // 2
+    me = me_ref[0]
+
+    def start_col(step):
+        piece = step // per
+        target = me ^ ((1 - piece // half) + 2 * (piece % half))
+        return pl.multiple_of(target * cols + (step % per) * tile, tile)
+
+    def copy_of(step, slot):
+        return pltpu.make_async_copy(
+            wd.at[0, :, pl.ds(start_col(step), tile)], buf.at[slot], sem.at[slot]
+        )
+
+    for step in range(slots):
+        copy_of(step, step).start()
+
+    each = share // 128
+
+    def load_pair(pair):
+        lane = pl.multiple_of((pair % each) * 128, 128)
+        return arrived[pair // each, :, pl.ds(lane, 128)].astype(F32)
+
+    for pair in range(hid // 128):
+        mine[:, pl.ds(pair * 128, 128)] = place(
+            load_pair, take_ref[2 * pair], take_ref[2 * pair + 1]
+        )
+    mask_all = mask_ref[...].astype(F32).astype(BF)
+
+    def product(step):
+        slot = lax.rem(step, slots)
+        spread = (
+            lax.broadcasted_iota(jnp.int32, (out_blocks, tile), 0)
+            == (start_col(step) + lax.broadcasted_iota(jnp.int32, (out_blocks, tile), 1)) // width
+        ).astype(BF)
+        mask = jnp.dot(mask_all, spread, preferred_element_type=F32).astype(BF)
+        copy_of(step, slot).wait()
+        weight = (buf[slot].reshape(blocks, width, tile) * mask[:, None, :]).reshape(hid, tile)
+        result = jnp.dot(mine[...], weight, preferred_element_type=F32)
+
+        @pl.when(step + slots < steps)
+        def _():
+            copy_of(step + slots, slot).start()
+
+        return result
+
+    def pass_body(step, carry):
+        part = pl.multiple_of((step % per) * tile, tile)
+        pass_ref[step // per, :, pl.ds(part, tile)] = product(step).astype(BF)
+        return carry
+
+    def keep_body(step, carry):
+        part = pl.multiple_of((step % per) * tile, tile)
+        keep_ref[step // per - half, :, pl.ds(part, tile)] = product(step)
+        return carry
+
+    lax.fori_loop(0, steps // 2, pass_body, 0)
+    lax.fori_loop(steps // 2, steps, keep_body, 0)
+    keep_ref[0] += x_ref[...].astype(F32)
+
+
+def down(me, take, arrived, x_own, mask, w_down):
+    pieces, rows, share = arrived.shape
+    hid, depth = w_down.shape[1:]
+    tile, slots = 512, 4
+    half = (pieces // 2, rows, depth // pieces)
+    return pl.pallas_call(
+        functools.partial(down_kernel, tile, slots),
+        in_specs=[SM, SM, VM, VM, VM, HB],
+        out_specs=(VM, VM),
+        out_shape=(jax.ShapeDtypeStruct(half, F32), jax.ShapeDtypeStruct(half, BF)),
+        scratch_shapes=[
+            pltpu.VMEM((slots, hid, tile), BF),
+            pltpu.SemaphoreType.DMA((slots,)),
+            pltpu.VMEM((rows, hid), BF),
+        ],
+        compiler_params=pltpu.CompilerParams(vmem_limit_bytes=32 * MIB),
+        cost_estimate=pl.CostEstimate(
+            flops=2 * rows * depth * hid, bytes_accessed=2 * depth * hid, transcendentals=0
+        ),
+        name="down",
+    )(me, take, arrived, x_own, mask, w_down)
+
+
+def partner(block, distance):
+    devices = range(lax.axis_size("tp"))
+    return lax.ppermute(block, "tp", [(i, i ^ distance) for i in devices])
+
+
+def onward(block, distance):
+    tp_count = lax.axis_size("tp")
+    sections = lax.axis_size("section")
+    route = [
+        (s * tp_count + t, (s + 1) % sections * tp_count + (t ^ distance))
+        for s in range(sections)
+        for t in range(tp_count)
+    ]
+    return lax.ppermute(block, ("section", "tp"), route)
+
+
+def gathered(own):
+    chips = lax.axis_size("tp") // 2
+    near = jnp.stack([own] + [partner(own, 2 * k) for k in range(1, chips)])
+    return jnp.concatenate([near, partner(near, 1)])
+
+
+def exchanged(blocks):
+    chips = blocks.shape[0] // 2
+    share = blocks.shape[2]
+    both = jnp.concatenate([blocks[:chips], partner(blocks[chips:], 1)], axis=2)
+    got = jnp.stack([both[0]] + [partner(both[k], 2 * k) for k in range(1, chips)])
+    return jnp.concatenate([got[:, :, :share], got[:, :, share:]])
+
+
+def body(
+    tokens,
+    norm_gain,
+    gate_weight,
+    up_weight,
+    gate_mask,
+    up_mask,
+    down_weight,
+    down_mask,
+    slot_order,
+):
+    sections = lax.axis_size("section")
+    tp_count = lax.axis_size("tp")
+    section_pos = lax.axis_index("section")
+    tp_pos = lax.axis_index("tp")
+    my_blocks = slot_order[0]
+    per_device = my_blocks.shape[0]
+    chips = tp_count // 2
+    capacity = per_device // tp_count
+    me = tp_pos.astype(jnp.int32).reshape(1)
+
+    places = jnp.arange(tp_count, dtype=jnp.int32)
+    away = places // chips + 2 * (places % chips)
+    lanes = jnp.arange(per_device, dtype=jnp.int32)
+    orders = lax.all_gather(my_blocks, "tp", axis=0)
+    mine_there = orders // per_device == tp_pos
+    ahead = lanes[None, :] < lanes[:, None]
+    rank_there = jnp.sum(
+        (mine_there[:, None, :] & ahead[None]).astype(jnp.int32), axis=2
+    )
+    ranks = jnp.arange(capacity, dtype=jnp.int32)
+    picked = mine_there[:, None, :] & (rank_there[:, None, :] == ranks[None, :, None])
+    to_send = jnp.sum(jnp.where(picked, orders[:, None, :] % per_device, 0), axis=2)
+    at_place = (tp_pos ^ away)[:, None] == places[None, :]
+    send = jnp.sum(jnp.where(at_place[:, :, None], to_send[None], 0), axis=1).reshape(-1)
+
+    origin = my_blocks // per_device
+    same = (origin[None, :] == origin[:, None]) & ahead
+    rank = jnp.sum(same.astype(jnp.int32), axis=1)
+    apart = origin ^ tp_pos
+    take = (apart % 2 * chips + apart // 2) * capacity + rank
+
+    x = gathered(tokens)
+    saved = jnp.zeros(tokens.shape, BF)
+    for round_pos in range(sections):
+        blocks = gate_up(
+            me, send, x, norm_gain, gate_mask[0], up_mask[0], gate_weight, up_weight
+        )
+        arrived = exchanged(blocks)
+        kept, passed = down(me, take, arrived, x[0], down_mask[0], down_weight)
+        sums = (kept + partner(passed, 1).astype(F32)).astype(BF)
+        parts = [onward(sums[k], 2 * k).astype(F32) for k in range(chips)]
+        own = functools.reduce(jnp.add, parts).astype(BF)
+        saved = jnp.where(section_pos == (round_pos + 1) % sections, own, saved)
+        if round_pos + 1 < sections:
+            x = gathered(own)
+    return saved[None]
+
+
 def solution(mesh):
+    tp_count = mesh.shape["tp"]
+    line_body = body if tp_count == 8 else ring_body
     return jax.shard_map(
-        body,
+        line_body,
         mesh=mesh,
         in_specs=(
             P(None, "tp"),

time: 749 us -> 341 us (0.46); the launches traced: 737 us -> 340 us
  matrix products: 188 us -> 0 us
  local copies, waits for them, and re-layouts: 166 us -> 4.07 us
  Pallas kernels: 0 us -> 140 us
  waiting for transfers between devices: 233 us -> 108 us
  other arithmetic: 85.5 us -> 4.68 us
  starting transfers between devices: 49.6 us -> 70.4 us
  between operations: 14.6 us -> 0.59 us
  blocking collectives: 0 us -> 12.8 us
    dot_general x12 -> x0, matrix products: 188 us -> none  [the longest x4 64.6 us: body(): partial_sum = jnp.dot(mine, w_down, preferred_element_type=jnp.float32)]
    pallas_call x0 -> x8, Pallas kernels: none -> 140 us  [the longest x4 88 us: gate_up(): pl.pallas_call(functools.partial(gate_up_kernel, tile, slots), in_specs=[...]
    reduce_scatter x4 -> x0, waiting for transfers between devices: 137 us -> none  [body(): lax.psum_scatter(partial_sum, 'tp', scatter_dimension=1, tiled=True)]
    unnamed x61 -> x25, local copies, waits for them, and re-layouts: 127 us -> 3.46 us
    ppermute x39 -> x52, waiting for transfers between devices: 37.6 us -> 108 us  [the longest x36 68.5 us: partner(): return lax.ppermute(block, 'tp', [(i, i ^ distance) for i in devices])]
    mul x3 -> x0, other arithmetic: 69.9 us -> none  [masked(): return weight * expand_mask(mask, width).astype(jnp.bfloat16)]
    all_gather x4 -> x0, waiting for transfers between devices: 58.4 us -> none  [the longest x3 58.4 us: body(): x_full = lax.all_gather(got_own, 'tp', axis=1, tiled=True)]
    gather x36 -> x0, local copies, waits for them, and re-layouts: 24.2 us -> none  [the longest x32 18.7 us: body(): outgoing = flat[send_lists[gather_offset]]]
  transfers between devices with their start and end apart: 47 -> 52, of which waited for: 26 -> 38; matrix products, arithmetic and copies ran while one was open for 30% -> 1% of each run, Pallas kernels for 0% -> 0%
where the time goes in v1:
time: 341 us; the launch traced here: 340 us
  Pallas kernels  140 us (41%)
  waiting for transfers between devices  108 us (32%)
  starting transfers between devices  70.4 us (21%)
  blocking collectives  12.8 us (4%)
  other arithmetic  4.68 us (1%)
  local copies, waits for them, and re-layouts  4.07 us (1%)
    pallas_call x4, Pallas kernels, gate_up(): pl.pallas_call(functools.partial(gate_up_kernel, tile, slots), in_specs=[...  88 us
    ppermute x36, waiting for transfers between devices, partner(): return lax.ppermute(block, 'tp', [(i, i ^ distance) for i in devices])  68.5 us
    pallas_call x4, Pallas kernels, down(): pl.pallas_call(functools.partial(down_kernel, tile, slots), in_specs=[SM,...  52.2 us
    ppermute x36, starting transfers between devices, partner(): return lax.ppermute(block, 'tp', [(i, i ^ distance) for i in devices])  39.6 us
    ppermute x16, waiting for transfers between devices, onward(): return lax.ppermute(block, ('section', 'tp'), route)  39 us
    ppermute x16, starting transfers between devices, onward(): return lax.ppermute(block, ('section', 'tp'), route)  30.8 us
    all_gather x1, blocking collectives, body(): orders = lax.all_gather(my_blocks, 'tp', axis=0)  12.8 us
  transfers between devices with their start and end apart: 52, of which 38 were waited for; matrix products, arithmetic and copies ran while one was open for 1% of the time, Pallas kernels for 0%

profile of v1, /device:TPU:0, one launch (start us, length us, event | category | flops | bytes accessed | tf_op | source)
XLA Modules:
  0.0 340.3 jit_solution(17300415461921856058)
XLA Ops:
  0.0 3.0 collective-permute-start
  5.6 12.8 %all-gather = s32[8,1,32]{2,1,0:T(1,128)S(1)} all-gather(s32[1,1,32]{2,1,0:T(1,128)} %bitcast.162), channel_id=1, replica_groups=mesh['section'=4,'tp'=8] {'tp'}, dimensions={0}, use_global_device_ids=true | all-gather | bytes 1152 | tf_op jit(solution)/shard_map/all_gather | solution.py:376
  26.2 22.0 %gate_up.4 = bf16[8,64,256]{2,1,0:T(8,128)(2,1)S(1)} custom-call(s32[1]{0:T(128)} %bitcast.me_ref, s32[32]{0:T(128)S(1)} %reshape.100.send_ref, bf16[8,64,1024]{2,1,0:T(8,128)(2,1)S(1)} %constant_dynamic-update-slice_fusion.x_ref, f32[1,8192]{1,0:T(1,128)S(1)} %copy-done.1, s32[128,32]{1,0:T(8,128)S(1)} %bitcast.123, s32[128,32]{1,0:T(8,128)S(1)} %bitcast.127, ...), custom_call_target="tpu_custom_call" | custom-call | flops 4294967296 | bytes 67108864 | tf_op jit(solution)/shard_map/gate_up/pallas_call | solution.py:208
  49.7 4.7 %collective-permute-start.7 = (bf16[64,512]{1,0:T(8,128)(2,1)S(1)}, bf16[64,512]{1,0:T(8,128)(2,1)S(1)}, u32[]{:S(2)}, u32[]{:S(2)}) collective-permute-start(bf16[64,512]{1,0:T(8,128)(2,1)S(1)} %get-tuple-element.71), channel_id=1, source_target_pairs={{0,6},{1,7},{2,4},{3,5},{4,2},{5,3},{6,0},{7,1},{8,14},{9,15},{10,... | collective-permute-start | bytes 196616 | tf_op jit(solution)/shard_map/ppermute | solution.py:324
  57.1 3.0 collective-permute-done.6
  60.3 13.0 %down.4 = (f32[4,64,1024]{2,1,0:T(8,128)S(1)}, bf16[4,64,1024]{2,1,0:T(8,128)(2,1)S(1)}) custom-call(s32[1]{0:T(128)} %bitcast.me_ref, s32[32]{0:T(128)S(1)} %multiply_add_fusion.take_ref, bf16[8,64,256]{2,1,0:T(8,128)(2,1)S(1)} %pad_maximum_fusion.5.arrived, bf16[64,1024]{1,0:T(8,128)(2,1)S(1)} %copy-done, s32[32,128]{1,0:T(8,128)S(1)} %bitcast.132, ...), custom_call_target="tpu_custom_call" | custom-call | flops 2147483648 | bytes 33554432 | tf_op jit(solution)/shard_map/down/pallas_call | solution.py:304
  75.5 3.6 %collective-permute-start.12 = (bf16[64,1024]{1,0:T(8,128)(2,1)S(1)}, bf16[64,1024]{1,0:T(8,128)(2,1)S(1)}, u32[]{:S(2)}, u32[]{:S(2)}) collective-permute-start(bf16[64,1024]{1,0:T(8,128)(2,1)S(1)} %get-tuple-element.40), channel_id=1, source_target_pairs={{0,14},{1,15},{2,12},{3,13},{4,10},{5,11},{6,8},{7,9},{8,22},{9,23... | collective-permute-start | bytes 393224 | tf_op jit(solution)/shard_map/ppermute | solution.py:335
  85.6 7.0 %collective-permute-done.11 = bf16[64,1024]{1,0:T(8,128)(2,1)S(1)} collective-permute-done((bf16[64,1024]{1,0:T(8,128)(2,1)S(1)}, bf16[64,1024]{1,0:T(8,128)(2,1)S(1)}, u32[]{:S(2)}, u32[]{:S(2)}) %collective-permute-start.11) | collective-permute-done | bytes 131104 | tf_op jit(solution)/shard_map/ppermute | solution.py:335
  99.6 8.1 %collective-permute-done.14 = bf16[64,1024]{1,0:T(8,128)(2,1)S(1)} collective-permute-done((bf16[64,1024]{1,0:T(8,128)(2,1)S(1)}, bf16[64,1024]{1,0:T(8,128)(2,1)S(1)}, u32[]{:S(2)}, u32[]{:S(2)}) %collective-permute-start.14) | collective-permute-done | bytes 131104 | tf_op jit(solution)/shard_map/ppermute | solution.py:324
  109.8 22.0 %gate_up.5 = bf16[8,64,256]{2,1,0:T(8,128)(2,1)S(1)} custom-call(s32[1]{0:T(128)} %bitcast.me_ref, s32[32]{0:T(128)S(1)} %reshape.100.send_ref, bf16[8,64,1024]{2,1,0:T(8,128)(2,1)S(1)} %constant_dynamic-update-slice_fusion.5.x_ref, f32[1,8192]{1,0:T(1,128)S(1)} %copy-done.2, s32[128,32]{1,0:T(8,128)S(1)} %bitcast.124, s32[128,32]{1,0:T(8,128)S(1)} %bitcast.128, ...), custom_call_target="tpu_custom_call" | custom-call | flops 4294967296 | bytes 67108864 | tf_op jit(solution)/shard_map/gate_up/pallas_call | solution.py:208
  134.9 2.6 collective-permute-start.19
  139.8 3.7 %collective-permute-done.19 = bf16[64,512]{1,0:T(8,128)(2,1)S(1)} collective-permute-done((bf16[64,512]{1,0:T(8,128)(2,1)S(1)}, bf16[64,512]{1,0:T(8,128)(2,1)S(1)}, u32[]{:S(2)}, u32[]{:S(2)}) %collective-permute-start.19) | collective-permute-done | bytes 65568 | tf_op jit(solution)/shard_map/ppermute | solution.py:324
  143.6 13.1 %down.5 = (f32[4,64,1024]{2,1,0:T(8,128)S(1)}, bf16[4,64,1024]{2,1,0:T(8,128)(2,1)S(1)}) custom-call(s32[1]{0:T(128)} %bitcast.me_ref, s32[32]{0:T(128)S(1)} %multiply_add_fusion.take_ref, bf16[8,64,256]{2,1,0:T(8,128)(2,1)S(1)} %pad_maximum_fusion.7.arrived, bf16[64,1024]{1,0:T(8,128)(2,1)S(1)} %get-tuple-element.26.x_ref, s32[32,128]{1,0:T(8,128)S(1)} %bitcast.133, ...), custom_call_target="tpu_custom_call" | custom-call | flops 2147483648 | bytes 33554432 | tf_op jit(solution)/shard_map/down/pallas_call | solution.py:304
  161.3 3.3 collective-permute-start.23
  169.1 4.7 %collective-permute-done.24 = bf16[64,1024]{1,0:T(8,128)(2,1)S(1)} collective-permute-done((bf16[64,1024]{1,0:T(8,128)(2,1)S(1)}, bf16[64,1024]{1,0:T(8,128)(2,1)S(1)}, u32[]{:S(2)}, u32[]{:S(2)}) %collective-permute-start.24) | collective-permute-done | bytes 131104 | tf_op jit(solution)/shard_map/ppermute | solution.py:335
  173.8 2.7 collective-permute-done.22
  181.0 2.7 collective-permute-done.26
  183.7 5.9 %collective-permute-done.27 = bf16[64,1024]{1,0:T(8,128)(2,1)S(1)} collective-permute-done((bf16[64,1024]{1,0:T(8,128)(2,1)S(1)}, bf16[64,1024]{1,0:T(8,128)(2,1)S(1)}, u32[]{:S(2)}, u32[]{:S(2)}) %collective-permute-start.27) | collective-permute-done | bytes 131104 | tf_op jit(solution)/shard_map/ppermute | solution.py:324
  191.7 22.0 %gate_up.6 = bf16[8,64,256]{2,1,0:T(8,128)(2,1)S(1)} custom-call(s32[1]{0:T(128)} %bitcast.me_ref, s32[32]{0:T(128)S(1)} %reshape.100.send_ref, bf16[8,64,1024]{2,1,0:T(8,128)(2,1)S(1)} %constant_dynamic-update-slice_fusion.10.x_ref, f32[1,8192]{1,0:T(1,128)S(1)} %copy-done.2, s32[128,32]{1,0:T(8,128)S(1)} %bitcast.125, s32[128,32]{1,0:T(8,128)S(1)} %bitcast.129, ...), custom_call_target="tpu_custom_call" | custom-call | flops 4294967296 | bytes 67108864 | tf_op jit(solution)/shard_map/gate_up/pallas_call | solution.py:208
  221.6 3.8 %collective-permute-done.32 = bf16[64,512]{1,0:T(8,128)(2,1)S(1)} collective-permute-done((bf16[64,512]{1,0:T(8,128)(2,1)S(1)}, bf16[64,512]{1,0:T(8,128)(2,1)S(1)}, u32[]{:S(2)}, u32[]{:S(2)}) %collective-permute-start.32) | collective-permute-done | bytes 65568 | tf_op jit(solution)/shard_map/ppermute | solution.py:324
  225.5 13.1 %down.6 = (f32[4,64,1024]{2,1,0:T(8,128)S(1)}, bf16[4,64,1024]{2,1,0:T(8,128)(2,1)S(1)}) custom-call(s32[1]{0:T(128)} %bitcast.me_ref, s32[32]{0:T(128)S(1)} %multiply_add_fusion.take_ref, bf16[8,64,256]{2,1,0:T(8,128)(2,1)S(1)} %pad_maximum_fusion.9.arrived, bf16[64,1024]{1,0:T(8,128)(2,1)S(1)} %get-tuple-element.24.x_ref, s32[32,128]{1,0:T(8,128)S(1)} %bitcast.134, ...), custom_call_target="tpu_custom_call" | custom-call | flops 2147483648 | bytes 33554432 | tf_op jit(solution)/shard_map/down/pallas_call | solution.py:304
  242.9 2.8 collective-permute-start.36
  245.7 2.8 collective-permute-start.35
  250.9 4.4 %collective-permute-done.37 = bf16[64,1024]{1,0:T(8,128)(2,1)S(1)} collective-permute-done((bf16[64,1024]{1,0:T(8,128)(2,1)S(1)}, bf16[64,1024]{1,0:T(8,128)(2,1)S(1)}, u32[]{:S(2)}, u32[]{:S(2)}) %collective-permute-start.37) | collective-permute-done | bytes 131104 | tf_op jit(solution)/shard_map/ppermute | solution.py:335
  262.5 3.0 collective-permute-done.39
  265.4 5.7 %collective-permute-done.40 = bf16[64,1024]{1,0:T(8,128)(2,1)S(1)} collective-permute-done((bf16[64,1024]{1,0:T(8,128)(2,1)S(1)}, bf16[64,1024]{1,0:T(8,128)(2,1)S(1)}, u32[]{:S(2)}, u32[]{:S(2)}) %collective-permute-start.40) | collective-permute-done | bytes 131104 | tf_op jit(solution)/shard_map/ppermute | solution.py:324
  273.2 22.0 %gate_up.7 = bf16[8,64,256]{2,1,0:T(8,128)(2,1)S(1)} custom-call(s32[1]{0:T(128)} %bitcast.me_ref, s32[32]{0:T(128)S(1)} %reshape.100.send_ref, bf16[8,64,1024]{2,1,0:T(8,128)(2,1)S(1)} %constant_dynamic-update-slice_fusion.15.x_ref, f32[1,8192]{1,0:T(1,128)S(1)} %copy-done.2, s32[128,32]{1,0:T(8,128)S(1)} %bitcast.126, s32[128,32]{1,0:T(8,128)S(1)} %bitcast.130, ...), custom_call_target="tpu_custom_call" | custom-call | flops 4294967296 | bytes 67108864 | tf_op jit(solution)/shard_map/gate_up/pallas_call | solution.py:208
  302.8 4.0 %collective-permute-done.45 = bf16[64,512]{1,0:T(8,128)(2,1)S(1)} collective-permute-done((bf16[64,512]{1,0:T(8,128)(2,1)S(1)}, bf16[64,512]{1,0:T(8,128)(2,1)S(1)}, u32[]{:S(2)}, u32[]{:S(2)}) %collective-permute-start.45) | collective-permute-done | bytes 65568 | tf_op jit(solution)/shard_map/ppermute | solution.py:324
  307.0 13.1 %down.7 = (f32[4,64,1024]{2,1,0:T(8,128)S(1)}, bf16[4,64,1024]{2,1,0:T(8,128)(2,1)S(1)}) custom-call(s32[1]{0:T(128)} %bitcast.me_ref, s32[32]{0:T(128)S(1)} %multiply_add_fusion.take_ref, bf16[8,64,256]{2,1,0:T(8,128)(2,1)S(1)} %pad_maximum_fusion.11.arrived, bf16[64,1024]{1,0:T(8,128)(2,1)S(1)} %get-tuple-element.22.x_ref, s32[32,128]{1,0:T(8,128)S(1)} %bitcast.135, ...), custom_call_target="tpu_custom_call" | custom-call | flops 2147483648 | bytes 33554432 | tf_op jit(solution)/shard_map/down/pallas_call | solution.py:304
  326.9 3.0 collective-permute-start.48
  332.5 4.4 %collective-permute-done.50 = bf16[64,1024]{1,0:T(8,128)(2,1)S(1)} collective-permute-done((bf16[64,1024]{1,0:T(8,128)(2,1)S(1)}, bf16[64,1024]{1,0:T(8,128)(2,1)S(1)}, u32[]{:S(2)}, u32[]{:S(2)}) %collective-permute-start.50) | collective-permute-done | bytes 131104 | tf_op jit(solution)/shard_map/ppermute | solution.py:335
  336.8 2.7 collective-permute-done.48
  (160 shorter events, 95.2 us)
Async XLA Ops:
  0.0 22.4 %collective-permute-start = (bf16[64,1024]{1,0:T(8,128)(2,1)}, bf16[64,1024]{1,0:T(8,128)(2,1)S(1)}, u32[]{:S(2)}, u32[]{:S(2)}) collective-permute-start(bf16[64,1024]{1,0:T(8,128)(2,1)} %x_ref.1), channel_id=1, source_target_pairs={{0,2},{1,3},{2,0},{3,1},{4,6},{5,7},{6,4},{7,5},{8,10},{9,11},{10,... | collective-permute-start | bytes 393224 | tf_op jit(solution)/shard_map/ppermute | solution.py:324
  3.0 19.4 %collective-permute-start.1 = (bf16[64,1024]{1,0:T(8,128)(2,1)}, bf16[64,1024]{1,0:T(8,128)(2,1)S(1)}, u32[]{:S(2)}, u32[]{:S(2)}) collective-permute-start(bf16[64,1024]{1,0:T(8,128)(2,1)} %x_ref.1), channel_id=1, source_target_pairs={{0,4},{1,5},{2,6},{3,7},{4,0},{5,1},{6,2},{7,3},{8,12},{9,13},{10,... | collective-permute-start | bytes 393224 | tf_op jit(solution)/shard_map/ppermute | solution.py:324
  5.6 16.8 %collective-permute-start.2 = (bf16[64,1024]{1,0:T(8,128)(2,1)}, bf16[64,1024]{1,0:T(8,128)(2,1)S(1)}, u32[]{:S(2)}, u32[]{:S(2)}) collective-permute-start(bf16[64,1024]{1,0:T(8,128)(2,1)} %x_ref.1), channel_id=1, source_target_pairs={{0,6},{1,7},{2,4},{3,5},{4,2},{5,3},{6,0},{7,1},{8,14},{9,15},{10,... | collective-permute-start | bytes 393224 | tf_op jit(solution)/shard_map/ppermute | solution.py:324
  49.7 7.4 %collective-permute-start.7 = (bf16[64,512]{1,0:T(8,128)(2,1)S(1)}, bf16[64,512]{1,0:T(8,128)(2,1)S(1)}, u32[]{:S(2)}, u32[]{:S(2)}) collective-permute-start(bf16[64,512]{1,0:T(8,128)(2,1)S(1)} %get-tuple-element.71), channel_id=1, source_target_pairs={{0,6},{1,7},{2,4},{3,5},{4,2},{5,3},{6,0},{7,1},{8,14},{9,15},{10,... | collective-permute-start | bytes 196616 | tf_op jit(solution)/shard_map/ppermute | solution.py:324
  75.5 10.1 %collective-permute-start.12 = (bf16[64,1024]{1,0:T(8,128)(2,1)S(1)}, bf16[64,1024]{1,0:T(8,128)(2,1)S(1)}, u32[]{:S(2)}, u32[]{:S(2)}) collective-permute-start(bf16[64,1024]{1,0:T(8,128)(2,1)S(1)} %get-tuple-element.40), channel_id=1, source_target_pairs={{0,14},{1,15},{2,12},{3,13},{4,10},{5,11},{6,8},{7,9},{8,22},{9,23... | collective-permute-start | bytes 393224 | tf_op jit(solution)/shard_map/ppermute | solution.py:335
  79.2 13.4 %collective-permute-start.11 = (bf16[64,1024]{1,0:T(8,128)(2,1)S(1)}, bf16[64,1024]{1,0:T(8,128)(2,1)S(1)}, u32[]{:S(2)}, u32[]{:S(2)}) collective-permute-start(bf16[64,1024]{1,0:T(8,128)(2,1)S(1)} %get-tuple-element.41), channel_id=1, source_target_pairs={{0,12},{1,13},{2,14},{3,15},{4,8},{5,9},{6,10},{7,11},{8,20},{9,21... | collective-permute-start | bytes 393224 | tf_op jit(solution)/shard_map/ppermute | solution.py:335
  80.3 12.3 %collective-permute-start.10 = (bf16[64,1024]{1,0:T(8,128)(2,1)S(1)}, bf16[64,1024]{1,0:T(8,128)(2,1)S(1)}, u32[]{:S(2)}, u32[]{:S(2)}) collective-permute-start(bf16[64,1024]{1,0:T(8,128)(2,1)S(1)} %get-tuple-element.42), channel_id=1, source_target_pairs={{0,10},{1,11},{2,8},{3,9},{4,14},{5,15},{6,12},{7,13},{8,18},{9,19... | collective-permute-start | bytes 393224 | tf_op jit(solution)/shard_map/ppermute | solution.py:335
  82.8 10.6 %collective-permute-start.9 = (bf16[64,1024]{1,0:T(8,128)(2,1)S(1)}, bf16[64,1024]{1,0:T(8,128)(2,1)S(1)}, u32[]{:S(2)}, u32[]{:S(2)}) collective-permute-start(bf16[64,1024]{1,0:T(8,128)(2,1)S(1)} %get-tuple-element.39), channel_id=1, source_target_pairs={{0,8},{1,9},{2,10},{3,11},{4,12},{5,13},{6,14},{7,15},{8,16},{9,17... | collective-permute-start | bytes 393224 | tf_op jit(solution)/shard_map/ppermute | solution.py:335
  95.6 12.2 %collective-permute-start.14 = (bf16[64,1024]{1,0:T(8,128)(2,1)S(1)}, bf16[64,1024]{1,0:T(8,128)(2,1)S(1)}, u32[]{:S(2)}, u32[]{:S(2)}) collective-permute-start(bf16[64,1024]{1,0:T(8,128)(2,1)S(1)} %get-tuple-element.26.x_ref), channel_id=1, source_target_pairs={{0,4},{1,5},{2,6},{3,7},{4,0},{5,1},{6,2},{7,3},{8,12},{9,13},{10,... | collective-permute-start | bytes 393224 | tf_op jit(solution)/shard_map/ppermute | solution.py:324
  96.6 11.2 %collective-permute-start.15 = (bf16[64,1024]{1,0:T(8,128)(2,1)S(1)}, bf16[64,1024]{1,0:T(8,128)(2,1)S(1)}, u32[]{:S(2)}, u32[]{:S(2)}) collective-permute-start(bf16[64,1024]{1,0:T(8,128)(2,1)S(1)} %get-tuple-element.26.x_ref), channel_id=1, source_target_pairs={{0,6},{1,7},{2,4},{3,5},{4,2},{5,3},{6,0},{7,1},{8,14},{9,15},{10,... | collective-permute-start | bytes 393224 | tf_op jit(solution)/shard_map/ppermute | solution.py:324
  133.3 6.5 %collective-permute-start.20 = (bf16[64,512]{1,0:T(8,128)(2,1)S(1)}, bf16[64,512]{1,0:T(8,128)(2,1)S(1)}, u32[]{:S(2)}, u32[]{:S(2)}) collective-permute-start(bf16[64,512]{1,0:T(8,128)(2,1)S(1)} %get-tuple-element.63), channel_id=1, source_target_pairs={{0,6},{1,7},{2,4},{3,5},{4,2},{5,3},{6,0},{7,1},{8,14},{9,15},{10,... | collective-permute-start | bytes 196616 | tf_op jit(solution)/shard_map/ppermute | solution.py:324
  134.9 8.7 %collective-permute-start.19 = (bf16[64,512]{1,0:T(8,128)(2,1)S(1)}, bf16[64,512]{1,0:T(8,128)(2,1)S(1)}, u32[]{:S(2)}, u32[]{:S(2)}) collective-permute-start(bf16[64,512]{1,0:T(8,128)(2,1)S(1)} %get-tuple-element.64), channel_id=1, source_target_pairs={{0,4},{1,5},{2,6},{3,7},{4,0},{5,1},{6,2},{7,3},{8,12},{9,13},{10,... | collective-permute-start | bytes 196616 | tf_op jit(solution)/shard_map/ppermute | solution.py:324
  158.9 10.2 %collective-permute-start.25 = (bf16[64,1024]{1,0:T(8,128)(2,1)S(1)}, bf16[64,1024]{1,0:T(8,128)(2,1)S(1)}, u32[]{:S(2)}, u32[]{:S(2)}) collective-permute-start(bf16[64,1024]{1,0:T(8,128)(2,1)S(1)} %get-tuple-element.36), channel_id=1, source_target_pairs={{0,14},{1,15},{2,12},{3,13},{4,10},{5,11},{6,8},{7,9},{8,22},{9,23... | collective-permute-start | bytes 393224 | tf_op jit(solution)/shard_map/ppermute | solution.py:335
  160.3 13.4 %collective-permute-start.24 = (bf16[64,1024]{1,0:T(8,128)(2,1)S(1)}, bf16[64,1024]{1,0:T(8,128)(2,1)S(1)}, u32[]{:S(2)}, u32[]{:S(2)}) collective-permute-start(bf16[64,1024]{1,0:T(8,128)(2,1)S(1)} %get-tuple-element.37), channel_id=1, source_target_pairs={{0,12},{1,13},{2,14},{3,15},{4,8},{5,9},{6,10},{7,11},{8,20},{9,21... | collective-permute-start | bytes 393224 | tf_op jit(solution)/shard_map/ppermute | solution.py:335
  161.3 12.5 %collective-permute-start.23 = (bf16[64,1024]{1,0:T(8,128)(2,1)S(1)}, bf16[64,1024]{1,0:T(8,128)(2,1)S(1)}, u32[]{:S(2)}, u32[]{:S(2)}) collective-permute-start(bf16[64,1024]{1,0:T(8,128)(2,1)S(1)} %get-tuple-element.38), channel_id=1, source_target_pairs={{0,10},{1,11},{2,8},{3,9},{4,14},{5,15},{6,12},{7,13},{8,18},{9,19... | collective-permute-start | bytes 393224 | tf_op jit(solution)/shard_map/ppermute | solution.py:335
  164.6 11.9 %collective-permute-start.22 = (bf16[64,1024]{1,0:T(8,128)(2,1)S(1)}, bf16[64,1024]{1,0:T(8,128)(2,1)S(1)}, u32[]{:S(2)}, u32[]{:S(2)}) collective-permute-start(bf16[64,1024]{1,0:T(8,128)(2,1)S(1)} %get-tuple-element.35), channel_id=1, source_target_pairs={{0,8},{1,9},{2,10},{3,11},{4,12},{5,13},{6,14},{7,15},{8,16},{9,17... | collective-permute-start | bytes 393224 | tf_op jit(solution)/shard_map/ppermute | solution.py:335
  176.6 7.2 %collective-permute-start.26 = (bf16[64,1024]{1,0:T(8,128)(2,1)S(1)}, bf16[64,1024]{1,0:T(8,128)(2,1)S(1)}, u32[]{:S(2)}, u32[]{:S(2)}) collective-permute-start(bf16[64,1024]{1,0:T(8,128)(2,1)S(1)} %get-tuple-element.24.x_ref), channel_id=1, source_target_pairs={{0,2},{1,3},{2,0},{3,1},{4,6},{5,7},{6,4},{7,5},{8,10},{9,11},{10,... | collective-permute-start | bytes 393224 | tf_op jit(solution)/shard_map/ppermute | solution.py:324
  176.6 13.0 %collective-permute-start.27 = (bf16[64,1024]{1,0:T(8,128)(2,1)S(1)}, bf16[64,1024]{1,0:T(8,128)(2,1)S(1)}, u32[]{:S(2)}, u32[]{:S(2)}) collective-permute-start(bf16[64,1024]{1,0:T(8,128)(2,1)S(1)} %get-tuple-element.24.x_ref), channel_id=1, source_target_pairs={{0,4},{1,5},{2,6},{3,7},{4,0},{5,1},{6,2},{7,3},{8,12},{9,13},{10,... | collective-permute-start | bytes 393224 | tf_op jit(solution)/shard_map/ppermute | solution.py:324
  178.7 10.9 %collective-permute-start.28 = (bf16[64,1024]{1,0:T(8,128)(2,1)S(1)}, bf16[64,1024]{1,0:T(8,128)(2,1)S(1)}, u32[]{:S(2)}, u32[]{:S(2)}) collective-permute-start(bf16[64,1024]{1,0:T(8,128)(2,1)S(1)} %get-tuple-element.24.x_ref), channel_id=1, source_target_pairs={{0,6},{1,7},{2,4},{3,5},{4,2},{5,3},{6,0},{7,1},{8,14},{9,15},{10,... | collective-permute-start | bytes 393224 | tf_op jit(solution)/shard_map/ppermute | solution.py:324
  216.8 8.6 %collective-permute-start.32 = (bf16[64,512]{1,0:T(8,128)(2,1)S(1)}, bf16[64,512]{1,0:T(8,128)(2,1)S(1)}, u32[]{:S(2)}, u32[]{:S(2)}) collective-permute-start(bf16[64,512]{1,0:T(8,128)(2,1)S(1)} %get-tuple-element.56), channel_id=1, source_target_pairs={{0,4},{1,5},{2,6},{3,7},{4,0},{5,1},{6,2},{7,3},{8,12},{9,13},{10,... | collective-permute-start | bytes 196616 | tf_op jit(solution)/shard_map/ppermute | solution.py:324
  240.8 10.2 %collective-permute-start.38 = (bf16[64,1024]{1,0:T(8,128)(2,1)S(1)}, bf16[64,1024]{1,0:T(8,128)(2,1)S(1)}, u32[]{:S(2)}, u32[]{:S(2)}) collective-permute-start(bf16[64,1024]{1,0:T(8,128)(2,1)S(1)} %get-tuple-element.32), channel_id=1, source_target_pairs={{0,14},{1,15},{2,12},{3,13},{4,10},{5,11},{6,8},{7,9},{8,22},{9,23... | collective-permute-start | bytes 393224 | tf_op jit(solution)/shard_map/ppermute | solution.py:335
  241.3 14.0 %collective-permute-start.37 = (bf16[64,1024]{1,0:T(8,128)(2,1)S(1)}, bf16[64,1024]{1,0:T(8,128)(2,1)S(1)}, u32[]{:S(2)}, u32[]{:S(2)}) collective-permute-start(bf16[64,1024]{1,0:T(8,128)(2,1)S(1)} %get-tuple-element.33), channel_id=1, source_target_pairs={{0,12},{1,13},{2,14},{3,15},{4,8},{5,9},{6,10},{7,11},{8,20},{9,21... | collective-permute-start | bytes 393224 | tf_op jit(solution)/shard_map/ppermute | solution.py:335
  242.9 12.4 %collective-permute-start.36 = (bf16[64,1024]{1,0:T(8,128)(2,1)S(1)}, bf16[64,1024]{1,0:T(8,128)(2,1)S(1)}, u32[]{:S(2)}, u32[]{:S(2)}) collective-permute-start(bf16[64,1024]{1,0:T(8,128)(2,1)S(1)} %get-tuple-element.34), channel_id=1, source_target_pairs={{0,10},{1,11},{2,8},{3,9},{4,14},{5,15},{6,12},{7,13},{8,18},{9,19... | collective-permute-start | bytes 393224 | tf_op jit(solution)/shard_map/ppermute | solution.py:335
  245.7 12.3 %collective-permute-start.35 = (bf16[64,1024]{1,0:T(8,128)(2,1)S(1)}, bf16[64,1024]{1,0:T(8,128)(2,1)S(1)}, u32[]{:S(2)}, u32[]{:S(2)}) collective-permute-start(bf16[64,1024]{1,0:T(8,128)(2,1)S(1)} %get-tuple-element.31), channel_id=1, source_target_pairs={{0,8},{1,9},{2,10},{3,11},{4,12},{5,13},{6,14},{7,15},{8,16},{9,17... | collective-permute-start | bytes 393224 | tf_op jit(solution)/shard_map/ppermute | solution.py:335
  258.0 7.4 %collective-permute-start.39 = (bf16[64,1024]{1,0:T(8,128)(2,1)S(1)}, bf16[64,1024]{1,0:T(8,128)(2,1)S(1)}, u32[]{:S(2)}, u32[]{:S(2)}) collective-permute-start(bf16[64,1024]{1,0:T(8,128)(2,1)S(1)} %get-tuple-element.22.x_ref), channel_id=1, source_target_pairs={{0,2},{1,3},{2,0},{3,1},{4,6},{5,7},{6,4},{7,5},{8,10},{9,11},{10,... | collective-permute-start | bytes 393224 | tf_op jit(solution)/shard_map/ppermute | solution.py:324
  258.2 12.9 %collective-permute-start.40 = (bf16[64,1024]{1,0:T(8,128)(2,1)S(1)}, bf16[64,1024]{1,0:T(8,128)(2,1)S(1)}, u32[]{:S(2)}, u32[]{:S(2)}) collective-permute-start(bf16[64,1024]{1,0:T(8,128)(2,1)S(1)} %get-tuple-element.22.x_ref), channel_id=1, source_target_pairs={{0,4},{1,5},{2,6},{3,7},{4,0},{5,1},{6,2},{7,3},{8,12},{9,13},{10,... | collective-permute-start | bytes 393224 | tf_op jit(solution)/shard_map/ppermute | solution.py:324
  260.5 10.6 %collective-permute-start.41 = (bf16[64,1024]{1,0:T(8,128)(2,1)S(1)}, bf16[64,1024]{1,0:T(8,128)(2,1)S(1)}, u32[]{:S(2)}, u32[]{:S(2)}) collective-permute-start(bf16[64,1024]{1,0:T(8,128)(2,1)S(1)} %get-tuple-element.22.x_ref), channel_id=1, source_target_pairs={{0,6},{1,7},{2,4},{3,5},{4,2},{5,3},{6,0},{7,1},{8,14},{9,15},{10,... | collective-permute-start | bytes 393224 | tf_op jit(solution)/shard_map/ppermute | solution.py:324
  298.6 8.3 %collective-permute-start.45 = (bf16[64,512]{1,0:T(8,128)(2,1)S(1)}, bf16[64,512]{1,0:T(8,128)(2,1)S(1)}, u32[]{:S(2)}, u32[]{:S(2)}) collective-permute-start(bf16[64,512]{1,0:T(8,128)(2,1)S(1)} %get-tuple-element.48), channel_id=1, source_target_pairs={{0,4},{1,5},{2,6},{3,7},{4,0},{5,1},{6,2},{7,3},{8,12},{9,13},{10,... | collective-permute-start | bytes 196616 | tf_op jit(solution)/shard_map/ppermute | solution.py:324
  322.2 10.2 %collective-permute-start.51 = (bf16[64,1024]{1,0:T(8,128)(2,1)S(1)}, bf16[64,1024]{1,0:T(8,128)(2,1)S(1)}, u32[]{:S(2)}, u32[]{:S(2)}) collective-permute-start(bf16[64,1024]{1,0:T(8,128)(2,1)S(1)} %get-tuple-element.28), channel_id=1, source_target_pairs={{0,14},{1,15},{2,12},{3,13},{4,10},{5,11},{6,8},{7,9},{8,22},{9,23... | collective-permute-start | bytes 393224 | tf_op jit(solution)/shard_map/ppermute | solution.py:335
  322.9 14.0 %collective-permute-start.50 = (bf16[64,1024]{1,0:T(8,128)(2,1)S(1)}, bf16[64,1024]{1,0:T(8,128)(2,1)S(1)}, u32[]{:S(2)}, u32[]{:S(2)}) collective-permute-start(bf16[64,1024]{1,0:T(8,128)(2,1)S(1)} %get-tuple-element.29), channel_id=1, source_target_pairs={{0,12},{1,13},{2,14},{3,15},{4,8},{5,9},{6,10},{7,11},{8,20},{9,21... | collective-permute-start | bytes 393224 | tf_op jit(solution)/shard_map/ppermute | solution.py:335
  324.5 12.3 %collective-permute-start.49 = (bf16[64,1024]{1,0:T(8,128)(2,1)S(1)}, bf16[64,1024]{1,0:T(8,128)(2,1)S(1)}, u32[]{:S(2)}, u32[]{:S(2)}) collective-permute-start(bf16[64,1024]{1,0:T(8,128)(2,1)S(1)} %get-tuple-element.30), channel_id=1, source_target_pairs={{0,10},{1,11},{2,8},{3,9},{4,14},{5,15},{6,12},{7,13},{8,18},{9,19... | collective-permute-start | bytes 393224 | tf_op jit(solution)/shard_map/ppermute | solution.py:335
  326.9 12.6 %collective-permute-start.48 = (bf16[64,1024]{1,0:T(8,128)(2,1)S(1)}, bf16[64,1024]{1,0:T(8,128)(2,1)S(1)}, u32[]{:S(2)}, u32[]{:S(2)}) collective-permute-start(bf16[64,1024]{1,0:T(8,128)(2,1)S(1)} %get-tuple-element.27), channel_id=1, source_target_pairs={{0,8},{1,9},{2,10},{3,11},{4,12},{5,13},{6,14},{7,15},{8,16},{9,17... | collective-permute-start | bytes 393224 | tf_op jit(solution)/shard_map/ppermute | solution.py:335
  (25 other events, 223.4 us)
